TPU v7x, 32 devices: a whole 2x2x4 slice. The times are simulated.
32 devices in a mesh: groups: 2 (over x), band: 16 (over z, y, core).
Axes of the slice: x: 2, y: 2, z: 4, core: 2. Of those that a mesh axis runs over, the one named last changes fastest.
Arguments:
- factor: bfloat16 [32768, 128], P(('groups', 'band')), parts along dimension 0
- near_vals: bfloat16 [512, 5, 64, 64], P(('groups', 'band')), parts along dimension 0, may hold values from 0.049804688 to 4
- far_vals: bfloat16 [32768, 512], P(('groups', 'band')), parts along dimension 0, may hold values from 0.049804688 to 4
- pub_rows: int32 [32, 32], P(('groups', 'band')), parts along dimension 0, may hold values from 0 to 1023
- far_count: int32 [32, 16], P(('groups', 'band')), parts along dimension 0, may hold values from 1 to 32, as said below
Outputs:
- updated: float32 [32768, 128], P(('groups', 'band')), parts along dimension 0
There are 2 independent parts, one for each index of `groups`. A program takes and returns all parts, laid end to end along the dimension named above; each array names one. Nothing has to cross between parts.
Inputs may be any that keep to these rules, and one draw needn't show every extreme that they name: `far_count`: in every row some entry equals 32.
All inputs are finite; a program needn't handle non-finite values.
Results may differ from a plain program's by a relative error of at most 0.0003.
Values may be sent and summed in bfloat16 or wider, within the bound.
A program may use at most 64 MiB of HBM per device.

v0:
```python
import jax
import jax.numpy as jnp
from jax import lax
from jax.sharding import PartitionSpec as P

BLOCK = 64
HALF_BLOCKS = 2


def extended(shard, sides, width):
    for axis, dim in sides:
        peers, length = (lax.axis_size(axis), shard.shape[dim])
        up = [(i, (i + 1) % peers) for i in range(peers - 1)]
        down = [(j, i) for i, j in up]
        last = lax.slice_in_dim(shard, length - width, length, axis=dim)
        first = lax.slice_in_dim(shard, 0, width, axis=dim)
        before = lax.ppermute(last, axis, up)
        after = lax.ppermute(first, axis, down)
        shard = jnp.concatenate([before, shard, after], axis=dim)
    return shard


def shards(factor, near_vals, far_vals, pub_rows, far_count):
    row_count, rank_width = factor.shape
    band_size = lax.axis_size("band")
    margin = HALF_BLOCKS * BLOCK
    padded = extended(factor, (("band", 0),), margin)
    block_count = row_count // BLOCK
    blocks = padded.reshape(block_count + 2 * HALF_BLOCKS, BLOCK, rank_width)
    near_sum = jnp.zeros((block_count, BLOCK, rank_width), jnp.float32)
    for offset in range(2 * HALF_BLOCKS + 1):
        near_sum = near_sum + jnp.einsum(
            "bij,bjk->bik",
            near_vals[:, offset],
            blocks[offset : offset + block_count],
            preferred_element_type=jnp.float32,
        )
    near_sum = near_sum.reshape(row_count, rank_width)
    slot_count = pub_rows.shape[1]
    chosen = jnp.take(factor, pub_rows[0], axis=0)
    slot_index = jnp.arange(band_size * slot_count, dtype=jnp.int32) % slot_count
    live_slots = slot_index < jnp.repeat(far_count[0], slot_count)
    masked = jnp.where(live_slots[None, :], far_vals, jnp.zeros((), far_vals.dtype))
    own_gram = lax.dot_general(
        factor, factor, (((0,), (0,)), ((), ())), preferred_element_type=jnp.float32
    )
    gram_matrix = lax.psum(own_gram, "band")
    arrived = lax.all_gather(chosen, "band", axis=0, tiled=True)
    far_sum = jnp.dot(masked, arrived, preferred_element_type=jnp.float32)
    lower_factor = jnp.linalg.cholesky(gram_matrix)
    inverse = jax.scipy.linalg.cho_solve(
        (lower_factor, True), jnp.eye(rank_width, dtype=jnp.float32)
    )
    return jnp.dot(near_sum + far_sum, inverse, precision=lax.Precision.HIGHEST)


def solution(mesh):
    placed = (
        P(("groups", "band"), None),
        P(("groups", "band"), None, None, None),
        P(("groups", "band"), None),
        P(("groups", "band"), None),
        P(("groups", "band"), None),
    )
    return jax.shard_map(
        shards, mesh=mesh, in_specs=placed, out_specs=P(("groups", "band"), None), check_vma=False
    )
```

profile of v0, /device:TPU:8, one launch (start us, length us, event | category | flops | bytes accessed | tf_op | source)
XLA Modules:
  0.0 138.6 jit_solution(12282025486069231995)
XLA Ops:
  6.5 0.0 copy-start
  6.5 0.0 all-reduce.2.cloned.1.call-start
  6.5 0.8 fusion.33
  7.4 1.9 %collective-permute-start = (bf16[128,128]{1,0:T(8,128)(2,1)S(1)}, bf16[128,128]{1,0:T(8,128)(2,1)S(1)}, u32[]{:S(2)}, u32[]{:S(2)}) collective-permute-start(bf16[128,128]{1,0:T(8,128)(2,1)S(1)} %get-tuple-element.11), channel_id=1, source_target_pairs={{0,1},{1,2},{2,3},{3,4},{4,5},{5,6},{6,7},{7,8},{8,9},{9,10},{10,1... | collective-permute-start | bytes 98312 | tf_op jit(solution)/shard_map/ppermute | solution.py:17
  9.3 4.5 %collective-permute-start.1 = (bf16[128,128]{1,0:T(8,128)(2,1)S(1)}, bf16[128,128]{1,0:T(8,128)(2,1)S(1)}, u32[]{:S(2)}, u32[]{:S(2)}) collective-permute-start(bf16[128,128]{1,0:T(8,128)(2,1)S(1)} %get-tuple-element.12), channel_id=1, source_target_pairs={{1,0},{2,1},{3,2},{4,3},{5,4},{6,5},{7,6},{8,7},{9,8},{10,9},{11,1... | collective-permute-start | bytes 98312 | tf_op jit(solution)/shard_map/ppermute | solution.py:18
  13.8 1.9 %fusion.34 = f32[128,128]{0,1:T(8,128)} fusion(bf16[1024,128]{1,0:T(8,128)(2,1)} %param.5), kind=kOutput, calls=%fused_computation.56 | convolution fusion | flops 33554432 | bytes 327680 | tf_op jit(solution)/shard_map/dot_general | solution.py:44
  15.8 0.0 all-reduce.2.cloned.1.call-update
  15.8 0.7 fusion.29
  16.5 0.7 compare_and_fusion
  17.1 1.6 %gather_fusion = bf16[32,128]{1,0:T(8,128)(2,1)S(1)} fusion(bf16[1024,128]{1,0:T(8,128)(2,1)} %param.5, s32[1024]{0:T(1024)S(1)} %pad_clamp_fusion), kind=kCustom, calls=%fused_computation | custom fusion | bytes 16512 | tf_op jit(solution)/shard_map/jit(_take)/gather | solution.py:40
  18.7 0.7 broadcast_in_dim.28
  19.4 0.1 reshape.74
  19.5 0.0 copy-start.1
  19.5 1.3 fusion.9
  20.9 0.1 broadcast_select_fusion
  20.9 19.7 %all_gather.3 = bf16[512,128]{1,0:T(8,128)(2,1)} all-gather(bf16[32,128]{1,0:T(8,128)(2,1)S(1)} %broadcast_select_fusion), channel_id=1, replica_groups=mesh['groups'=2,'band'=16] {'band'}, dimensions={0}, use_global_device_ids=true | all-gather | bytes 139264 | tf_op jit(solution)/shard_map/all_gather | solution.py:48
  40.6 0.0 collective-permute-done
  40.6 0.0 copy-done
  40.6 0.1 constant_dynamic-update-slice_fusion
  40.7 0.0 copy-done.1
  40.7 0.2 fusion.11
  40.9 0.0 collective-permute-done.1
  41.0 0.2 convolution_bitcast_fusion
  41.2 62.1 %all-reduce.2.cloned.1.call-done = f32[128,128]{0,1:T(8,128)} async-done(((f32[128,128]{0,1:T(8,128)}), f32[128,128]{0,1:T(8,128)}) %all-reduce.2.cloned.1.call-update) | async-done | bytes 65552 | tf_op jit(solution)/shard_map/psum | solution.py:47
  103.3 0.9 copy.12
  104.2 0.9 fusion.24
  105.1 11.7 %cholesky.17 = f32[128,128]{1,0:T(8,128)S(1)} custom-call(f32[128,128]{1,0:T(8,128)S(1)} %fusion.24), custom_call_target="Cholesky" | custom-call | tf_op jit(solution)/shard_map/jit(cholesky)/cholesky | solution.py:50
  116.8 0.6 compare_reduce_fusion
  117.5 0.7 fusion.19
  118.1 9.8 %custom-call.10 = f32[1,128,128]{1,2,0:T(8,128)S(1)} custom-call(f32[1,128,128]{2,1,0:T(8,128)S(1)} %fusion.19), custom_call_target="InvertDiagBlocksLowerTriangular" | custom-call | tf_op jit(solution)/shard_map/jit(_cho_solve)/triangular_solve | solution.py:51
  128.0 0.2 fusion.22
  128.2 0.2 fusion.20
  128.4 0.2 fusion.3
  128.6 0.0 copy-start.2
  128.7 0.0 copy-start.3
  128.7 0.2 fusion.1
  128.9 0.7 copy-done.2
  129.6 0.4 copy-done.3
  130.0 0.4 convolution_add_fusion
  130.4 1.4 fusion.35
  (7 shorter events, 0.1 us)
Async XLA Ops:
  6.5 34.1 %copy-start = (bf16[1024,128]{1,0:T(8,128)(2,1)S(1)}, bf16[1024,128]{1,0:T(8,128)(2,1)}, u32[]{:S(2)}) copy-start(bf16[1024,128]{1,0:T(8,128)(2,1)} %param.5) | copy-start | bytes 786436
  6.5 96.8 %all-reduce.2.cloned.1.call-start = ((), (), s32[]{:S(2)}) async-start(), calls=%async_computation | async-start | bytes 131072 | tf_op jit(solution)/shard_map/psum | solution.py:47
  7.4 33.2 %collective-permute-start = (bf16[128,128]{1,0:T(8,128)(2,1)S(1)}, bf16[128,128]{1,0:T(8,128)(2,1)S(1)}, u32[]{:S(2)}, u32[]{:S(2)}) collective-permute-start(bf16[128,128]{1,0:T(8,128)(2,1)S(1)} %get-tuple-element.11), channel_id=1, source_target_pairs={{0,1},{1,2},{2,3},{3,4},{4,5},{5,6},{6,7},{7,8},{8,9},{9,10},{10,1... | collective-permute-start | bytes 98312 | tf_op jit(solution)/shard_map/ppermute | solution.py:17
  9.3 31.7 %collective-permute-start.1 = (bf16[128,128]{1,0:T(8,128)(2,1)S(1)}, bf16[128,128]{1,0:T(8,128)(2,1)S(1)}, u32[]{:S(2)}, u32[]{:S(2)}) collective-permute-start(bf16[128,128]{1,0:T(8,128)(2,1)S(1)} %get-tuple-element.12), channel_id=1, source_target_pairs={{1,0},{2,1},{3,2},{4,3},{5,4},{6,5},{7,6},{8,7},{9,8},{10,9},{11,1... | collective-permute-start | bytes 98312 | tf_op jit(solution)/shard_map/ppermute | solution.py:18
  19.5 21.2 %copy-start.1 = (bf16[16,5,64,64]{3,2,1,0:T(8,128)(2,1)S(1)}, bf16[16,5,64,64]{3,2,1,0:T(8,128)(2,1)}, u32[]{:S(2)}) copy-start(bf16[16,5,64,64]{3,2,1,0:T(8,128)(2,1)} %param.6) | copy-start | bytes 1966084
  128.6 0.9 copy-start.2
  128.7 1.3 copy-start.3
Sparse Core Ops, SparseCore 0:
  15.9 87.3 all-reduce.1
where the time goes:
time: 139 us
  waiting for transfers between devices  62.1 us (45%)
  other arithmetic  25.1 us (18%)
  blocking collectives  19.7 us (14%)
  between operations  13.5 us (10%)
  starting transfers between devices  6.45 us (5%)
  matrix products  6.39 us (5%)
  local copies, waits for them, and re-layouts  5.35 us (4%)
    psum x1, waiting for transfers between devices, shards(): gram_matrix = lax.psum(own_gram, 'band')  62.1 us
    all_gather x1, blocking collectives, shards(): arrived = lax.all_gather(chosen, 'band', axis=0, tiled=True)  19.7 us
    another operation x3, other arithmetic, shards(): lower_factor = jnp.linalg.cholesky(gram_matrix)  12.4 us
    another operation x2, other arithmetic, shards(): jax.scipy.linalg.cho_solve((lower_factor, True), jnp.eye(rank_width, dtyp...  10.5 us
    ppermute x1, starting transfers between devices, extended(): after = lax.ppermute(first, axis, down)  4.54 us
  transfers between devices with their start and end apart: 3, of which 1 were waited for; matrix products, arithmetic and copies ran while one was open for 6% of the time, Pallas kernels for 0%

commit v1 on v0

--- a/solution.py
+++ b/solution.py
@@ -44,7 +44,7 @@
     own_gram = lax.dot_general(
         factor, factor, (((0,), (0,)), ((), ())), preferred_element_type=jnp.float32
     )
-    gram_matrix = lax.psum(own_gram, "band")
+    gram_matrix = jnp.sum(lax.all_gather(own_gram, "band"), axis=0)
     arrived = lax.all_gather(chosen, "band", axis=0, tiled=True)
     far_sum = jnp.dot(masked, arrived, preferred_element_type=jnp.float32)
     lower_factor = jnp.linalg.cholesky(gram_matrix)

time: 139 us -> 89 us (0.64)
  the two profiles are of different devices: /device:TPU:8 before, /device:TPU:0 now
where the time goes in v1:
time: 89 us; the launch traced here: 88.6 us
  other arithmetic  25.6 us (29%)
  blocking collectives  25.4 us (29%)
  between operations  13.5 us (15%)
  waiting for transfers between devices  8.67 us (10%)
  matrix products  6.27 us (7%)
  local copies, waits for them, and re-layouts  5.58 us (6%)
  starting transfers between devices  3.64 us (4%)
    all_gather x1, blocking collectives, shards(): arrived = lax.all_gather(chosen, 'band', axis=0, tiled=True)  25.4 us
    another operation x3, other arithmetic, shards(): lower_factor = jnp.linalg.cholesky(gram_matrix)  12.4 us
    another operation x2, other arithmetic, shards(): jax.scipy.linalg.cho_solve((lower_factor, True), jnp.eye(rank_width, dtyp...  10.5 us
    all_gather x1, waiting for transfers between devices, shards(): gram_matrix = jnp.sum(lax.all_gather(own_gram, 'band'), axis=0)  8.64 us
    ppermute x1, starting transfers between devices, extended(): before = lax.ppermute(last, axis, up)  2.35 us
    unnamed x7, local copies, waits for them, and re-layouts  2.15 us
    dot_general x5, matrix products, shards(): jnp.einsum('bij,bjk->bik', near_vals[:, offset], blocks[offset:offset + b...  2.09 us
    dot_general x1, matrix products, shards(): lax.dot_general(factor, factor, (((0,), (0,)), ((), ())), preferred_eleme...  1.93 us
  transfers between devices with their start and end apart: 3, of which 1 were waited for; matrix products, arithmetic and copies ran while one was open for 9% of the time, Pallas kernels for 0%

profile of v1, /device:TPU:0, one launch (start us, length us, event | category | flops | bytes accessed | tf_op | source)
XLA Modules:
  0.0 88.6 jit_solution(13593330854863612922)
XLA Ops:
  6.5 0.0 copy-start
  6.5 0.0 all-gather.3.cloned.1.call-start
  6.5 0.8 fusion.33
  7.4 2.3 %collective-permute-start = (bf16[128,128]{1,0:T(8,128)(2,1)S(1)}, bf16[128,128]{1,0:T(8,128)(2,1)S(1)}, u32[]{:S(2)}, u32[]{:S(2)}) collective-permute-start(bf16[128,128]{1,0:T(8,128)(2,1)S(1)} %get-tuple-element.11), channel_id=1, source_target_pairs={{0,1},{1,2},{2,3},{3,4},{4,5},{5,6},{6,7},{7,8},{8,9},{9,10},{10,1... | collective-permute-start | bytes 98312 | tf_op jit(solution)/shard_map/ppermute | solution.py:17
  9.7 1.3 %collective-permute-start.1 = (bf16[128,128]{1,0:T(8,128)(2,1)S(1)}, bf16[128,128]{1,0:T(8,128)(2,1)S(1)}, u32[]{:S(2)}, u32[]{:S(2)}) collective-permute-start(bf16[128,128]{1,0:T(8,128)(2,1)S(1)} %get-tuple-element.12), channel_id=1, source_target_pairs={{1,0},{2,1},{3,2},{4,3},{5,4},{6,5},{7,6},{8,7},{9,8},{10,9},{11,1... | collective-permute-start | bytes 98312 | tf_op jit(solution)/shard_map/ppermute | solution.py:18
  11.0 1.9 %fusion.34 = f32[128,128]{1,0:T(8,128)} fusion(bf16[1024,128]{1,0:T(8,128)(2,1)} %param.5), kind=kOutput, calls=%fused_computation.56 | convolution fusion | flops 33554432 | bytes 327680 | tf_op jit(solution)/shard_map/dot_general | solution.py:44
  13.0 0.0 all-gather.3.cloned.1.call-update
  13.0 0.7 fusion.29
  13.6 0.7 compare_and_fusion
  14.3 1.6 %gather_fusion = bf16[32,128]{1,0:T(8,128)(2,1)S(1)} fusion(bf16[1024,128]{1,0:T(8,128)(2,1)} %param.5, s32[1024]{0:T(1024)S(1)} %pad_clamp_fusion), kind=kCustom, calls=%fused_computation | custom fusion | bytes 16512 | tf_op jit(solution)/shard_map/jit(_take)/gather | solution.py:40
  15.9 0.7 broadcast_in_dim.28
  16.6 0.1 reshape.74
  16.7 1.2 %fusion.9 = f32[16,64,128]{2,1,0:T(8,128)S(1)} fusion(bf16[16,64,128]{2,1,0:T(8,128)(2,1)} %bitcast.73, bf16[16,5,64,64]{3,2,1,0:T(8,128)(2,1)} %param.6), kind=kOutput, calls=%fused_computation.14 | convolution fusion | flops 16777216 | bytes 1048576 | tf_op jit(solution)/shard_map/bij,bjk->bik/dot_general | solution.py:32
  17.9 0.1 broadcast_select_fusion
  18.0 25.4 %all_gather.9 = bf16[512,128]{1,0:T(8,128)(2,1)S(1)} all-gather(bf16[32,128]{1,0:T(8,128)(2,1)S(1)} %broadcast_select_fusion), channel_id=1, replica_groups=mesh['groups'=2,'band'=16] {'band'}, dimensions={0}, use_global_device_ids=true | all-gather | bytes 139264 | tf_op jit(solution)/shard_map/all_gather | solution.py:48
  43.4 0.0 collective-permute-done
  43.4 0.0 copy-done
  43.4 0.0 copy-start.1
  43.4 0.1 constant_dynamic-update-slice_fusion
  43.5 0.0 collective-permute-done.1
  43.6 1.1 %copy-done.1 = bf16[16,5,64,64]{3,2,1,0:T(8,128)(2,1)S(1)} copy-done((bf16[16,5,64,64]{3,2,1,0:T(8,128)(2,1)S(1)}, bf16[16,5,64,64]{3,2,1,0:T(8,128)(2,1)}, u32[]{:S(2)}) %copy-start.1) | copy-done | bytes 655384
  44.7 0.2 fusion.11
  44.9 0.2 convolution_bitcast_fusion
  45.2 0.2 fusion.3
  45.4 0.0 copy-start.2
  45.4 0.2 fusion.1
  45.6 1.0 %copy-done.2 = bf16[1024,512]{1,0:T(8,128)(2,1)S(1)} copy-done((bf16[1024,512]{1,0:T(8,128)(2,1)S(1)}, bf16[1024,512]{1,0:T(8,128)(2,1)}, u32[]{:S(2)}) %copy-start.2) | copy-done | bytes 1048600
  46.6 0.4 convolution_add_fusion
  47.0 8.6 %all-gather.3.cloned.1.call-done = f32[2048,128]{1,0:T(8,128)} async-done(((f32[128,128]{1,0:T(8,128)}), f32[2048,128]{1,0:T(8,128)}) %all-gather.3.cloned.1.call-update) | async-done | bytes 1048592 | tf_op jit(solution)/shard_map/all_gather | solution.py:47
  55.7 1.3 %reduce_sum.9 = f32[128,128]{1,0:T(8,128)S(1)} reduce(f32[16,128,128]{2,1,0:T(8,128)} %bitcast.74, f32[]{:T(128)} %constant.79.clone.1), dimensions={0}, to_apply=%region_0.1 | reduce | flops 245760 | bytes 1114116 | tf_op jit(solution)/shard_map/reduce_sum | solution.py:47
  57.0 0.1 copy.17
  57.1 11.7 %cholesky.17 = f32[128,128]{1,0:T(8,128)S(1)} custom-call(f32[128,128]{1,0:T(8,128)S(1)} %fusion.24), custom_call_target="Cholesky" | custom-call | tf_op jit(solution)/shard_map/jit(cholesky)/cholesky | solution.py:50
  68.8 0.6 compare_reduce_fusion
  69.5 0.7 fusion.19
  70.2 9.8 %custom-call.10 = f32[1,128,128]{1,2,0:T(8,128)S(1)} custom-call(f32[1,128,128]{2,1,0:T(8,128)S(1)} %fusion.19), custom_call_target="InvertDiagBlocksLowerTriangular" | custom-call | tf_op jit(solution)/shard_map/jit(_cho_solve)/triangular_solve | solution.py:51
  80.0 0.2 fusion.22
  80.2 0.2 fusion.20
  80.4 1.4 %fusion.35 = f32[1024,128]{1,0:T(8,128)} fusion(f32[1024,128]{1,0:T(8,128)S(1)} %convolution_add_fusion, f32[128,128]{1,0:T(8,128)S(1)} %fusion.20), kind=kOutput, calls=%fused_computation.57 | convolution fusion | flops 201326592 | bytes 1114112 | tf_op jit(solution)/shard_map/dot_general | solution.py:54
  (8 shorter events, 0.1 us)
Async XLA Ops:
  6.5 36.9 %copy-start = (bf16[1024,128]{1,0:T(8,128)(2,1)S(1)}, bf16[1024,128]{1,0:T(8,128)(2,1)}, u32[]{:S(2)}) copy-start(bf16[1024,128]{1,0:T(8,128)(2,1)} %param.5) | copy-start | bytes 786436
  6.5 49.2 %all-gather.3.cloned.1.call-start = ((), (), s32[]{:S(2)}) async-start(), calls=%async_computation | async-start | bytes 1114112 | tf_op jit(solution)/shard_map/all_gather | solution.py:47
  7.4 36.0 %collective-permute-start = (bf16[128,128]{1,0:T(8,128)(2,1)S(1)}, bf16[128,128]{1,0:T(8,128)(2,1)S(1)}, u32[]{:S(2)}, u32[]{:S(2)}) collective-permute-start(bf16[128,128]{1,0:T(8,128)(2,1)S(1)} %get-tuple-element.11), channel_id=1, source_target_pairs={{0,1},{1,2},{2,3},{3,4},{4,5},{5,6},{6,7},{7,8},{8,9},{9,10},{10,1... | collective-permute-start | bytes 98312 | tf_op jit(solution)/shard_map/ppermute | solution.py:17
  9.7 33.8 %collective-permute-start.1 = (bf16[128,128]{1,0:T(8,128)(2,1)S(1)}, bf16[128,128]{1,0:T(8,128)(2,1)S(1)}, u32[]{:S(2)}, u32[]{:S(2)}) collective-permute-start(bf16[128,128]{1,0:T(8,128)(2,1)S(1)} %get-tuple-element.12), channel_id=1, source_target_pairs={{1,0},{2,1},{3,2},{4,3},{5,4},{6,5},{7,6},{8,7},{9,8},{10,9},{11,1... | collective-permute-start | bytes 98312 | tf_op jit(solution)/shard_map/ppermute | solution.py:18
  43.4 1.3 %copy-start.1 = (bf16[16,5,64,64]{3,2,1,0:T(8,128)(2,1)S(1)}, bf16[16,5,64,64]{3,2,1,0:T(8,128)(2,1)}, u32[]{:S(2)}) copy-start(bf16[16,5,64,64]{3,2,1,0:T(8,128)(2,1)} %param.6) | copy-start | bytes 1966084
  45.4 1.2 %copy-start.2 = (bf16[1024,512]{1,0:T(8,128)(2,1)S(1)}, bf16[1024,512]{1,0:T(8,128)(2,1)}, u32[]{:S(2)}) copy-start(bf16[1024,512]{1,0:T(8,128)(2,1)} %param.7) | copy-start | bytes 3145732
Sparse Core Ops, SparseCore 0:
  13.1 42.5 all-gather.2
